TPU v7x, 32 devices: a whole 2x2x4 slice. The times are simulated.
32 devices in a mesh: band: 4 (over x, core), isdf: 8 (over z, y).
Axes of the slice: x: 2, y: 2, z: 4, core: 2. Of those that a mesh axis runs over, the one named last changes fastest.
Arguments:
- trial: bfloat16 [512, 2, 512], P('isdf', None, 'band'), may hold values from -6 to 6
- cond_coef: bfloat16 [512, 8192], P('band', 'isdf'), may hold values from -0.25 to 0.25
- val_coef: bfloat16 [512, 8192], P('band', 'isdf'), may hold values from -1.5 to 1.5
- kernel: bfloat16 [8192, 8192], P('isdf', 'band'), may hold values from -0.09375 to 0.09375
- block_mask: int32 [64, 64], P('isdf', 'band'), may hold values from 0 to 1, as said below
Outputs:
- sigma: bfloat16 [512, 2, 512], P('isdf', None, 'band')
Inputs may be any that keep to these rules, and one draw needn't show every extreme that they name: `block_mask`: 0 or 1; every block on the diagonal and within two blocks of it, cyclically, is 1.
All inputs are finite; a program needn't handle non-finite values.
Results may differ from a plain program's by a relative error of at most 0.0058.
Values may be sent and summed in bfloat16 or wider, within the bound.
A program may use at most 64 MiB of HBM per device.

v0:
```python
import jax
import jax.numpy as jnp
from jax import lax
from jax.sharding import PartitionSpec as P


def on_device(trial, cond_coef, val_coef, kernel, block_mask):
    trial_count = trial.shape[1]
    valence_dev = trial.shape[2]
    points_dev = val_coef.shape[1]
    width_pairs = trial_count * valence_dev
    cond_full = lax.all_gather(cond_coef, "band", axis=0, tiled=True)
    piece = lax.all_gather(trial, "isdf", axis=0, tiled=True)
    flat_piece = piece.reshape(piece.shape[0], width_pairs)
    orbitals = cond_full
    pairs = lax.dot_general(
        flat_piece, orbitals, (((0,), (0,)), ((), ())), preferred_element_type=jnp.float32
    )
    partial_proj = jnp.sum(
        pairs.reshape(trial_count, valence_dev, points_dev) * val_coef[None], axis=1
    )
    projected = lax.psum(partial_proj, "band")
    rounded = projected.astype(jnp.bfloat16)
    mask_rows = block_mask.shape[0]
    mask_cols = block_mask.shape[1]
    block_size = kernel.shape[0] // mask_rows
    shaped = kernel.reshape(mask_rows, block_size, mask_cols, block_size)
    masked = jnp.where(
        block_mask[:, None, :, None] > 0, shaped, jnp.zeros((), kernel.dtype)
    ).reshape(kernel.shape)
    screen_part = jnp.dot(rounded, masked, preferred_element_type=jnp.float32)
    screen_band = lax.psum(screen_part, "isdf")
    screen_full = lax.all_gather(screen_band, "band", axis=1, tiled=True)
    screen_local = lax.dynamic_slice_in_dim(
        screen_full, lax.axis_index("isdf") * points_dev, points_dev, 1
    )
    weighted = (
        (val_coef[None] * screen_local[:, None, :])
        .astype(jnp.bfloat16)
        .reshape(width_pairs, points_dev)
    )
    orbitals = cond_full
    summed = lax.psum_scatter(
        lax.dot_general(
            orbitals, weighted, (((1,), (1,)), ((), ())), preferred_element_type=jnp.float32
        ),
        "isdf",
        scatter_dimension=0,
        tiled=True,
    )
    return summed.reshape(trial.shape).astype(jnp.bfloat16)


def solution(mesh):
    return jax.shard_map(
        on_device,
        mesh=mesh,
        in_specs=(
            P("isdf", None, "band"),
            P("band", "isdf"),
            P("band", "isdf"),
            P("isdf", "band"),
            P("isdf", "band"),
        ),
        out_specs=P("isdf", None, "band"),
        check_vma=False,
    )
```

profile of v0, /device:TPU:0, one launch (start us, length us, event | category | flops | bytes accessed | tf_op | source)
XLA Modules:
  0.0 166.1 jit_solution(15147323869442083194)
XLA Ops:
  6.5 0.0 all-gather.2.cloned.1.call-start
  6.5 0.7 all-gather.2.cloned.1.call-update
  7.3 0.0 reduce-scatter.4.cloned.1.call-start
  7.3 32.7 %all_gather.9 = bf16[512,2,128]{2,1,0:T(2,128)(2,1)S(1)} all-gather(bf16[64,2,128]{2,1,0:T(2,128)(2,1)} %param.5), channel_id=1, replica_groups=mesh['band'=4,'isdf'=8] {'isdf'}, dimensions={0}, use_global_device_ids=true | all-gather | bytes 294912 | tf_op jit(solution)/shard_map/all_gather | solution.py:13
  40.0 0.2 copy.10
  40.2 1.0 convert_element_type.21
  41.2 0.7 broadcast_compare_fusion
  41.9 0.0 all-gather.2.cloned.1.call-done
  41.9 1.7 %fusion.2 = f32[2,1024]{1,0:T(2,128)S(1)} fusion(bf16[512,1024]{1,0:T(8,128)(2,1)} %all-gather.2.cloned.1.call-done, f32[128,1024]{1,0:T(8,128)S(1)} %convert_element_type.21, bf16[512,2,128]{0,2,1:T(8,128)(2,1)S(1)} %copy.10), kind=kOutput, calls=%fused_computation.4 | convolution fusion | flops 268957696 | bytes 1843200 | tf_op jit(solution)/shard_map/dot_general | solution.py:16
  43.6 5.8 %psum.14 = bf16[2,1024]{1,0:T(2,128)(2,1)S(1)} all-reduce(f32[2,1024]{1,0:T(2,128)S(1)} %fusion.2), channel_id=1, replica_groups=mesh['band'=4,'isdf'=8] {'band'}, use_global_device_ids=true, to_apply=%region_1.0 | all-reduce | flops 2048 | bytes 12288 | tf_op jit(solution)/shard_map/psum | solution.py:22
  49.4 0.6 broadcast_in_dim.18
  50.0 0.0 copy-start
  50.0 3.6 %fusion = f32[2,2048]{1,0:T(2,128)S(1)} fusion(bf16[1024,2048]{1,0:T(8,128)(2,1)} %param.8, pred[128,8,16,128]{3,2,1,0:T(8,128)(4,1)S(1)} %bitcast.23, bf16[2,1024]{1,0:T(2,128)(2,1)S(1)} %psum.14), kind=kOutput, calls=%fused_computation.1 | convolution fusion | flops 10485760 | bytes 6311936 | tf_op jit(solution)/shard_map/dot_general | solution.py:31
  53.6 37.2 %psum.15 = f32[2,2048]{1,0:T(2,128)S(1)} all-reduce(f32[2,2048]{1,0:T(2,128)S(1)} %fusion), channel_id=1, replica_groups=mesh['band'=4,'isdf'=8] {'isdf'}, use_global_device_ids=true, to_apply=%region_2.3 | all-reduce | flops 4096 | bytes 32768 | tf_op jit(solution)/shard_map/psum | solution.py:32
  90.8 5.2 %all_gather.11 = f32[2,8192]{1,0:T(2,128)S(1)} all-gather(f32[2,2048]{1,0:T(2,128)S(1)} %psum.15), channel_id=1, replica_groups=mesh['band'=4,'isdf'=8] {'band'}, dimensions={1}, use_global_device_ids=true | all-gather | bytes 81920 | tf_op jit(solution)/shard_map/all_gather | solution.py:33
  96.0 0.1 multiply_convert_fusion
  96.1 0.0 copy-done
  96.1 0.5 convolution_bitcast_fusion
  96.6 1.0 copy.11
  97.6 0.0 reduce-scatter.4.cloned.1.call-update
  97.6 60.0 %reduce-scatter.4.cloned.1.call-done = f32[64,256]{1,0:T(8,128)} async-done(((f32[512,256]{1,0:T(8,128)}), f32[64,256]{1,0:T(8,128)}) %reduce-scatter.4.cloned.1.call-update) | async-done | bytes 65552
  157.6 0.9 copy.12
  158.6 0.7 copy.9
  (1 shorter events, 0.0 us)
Async XLA Ops:
  6.5 35.4 %all-gather.2.cloned.1.call-start = ((), (), s32[]{:S(2)}) async-start(), calls=%async_computation.1 | async-start | bytes 1310720 | tf_op jit(solution)/shard_map/all_gather | solution.py:12
  7.3 150.4 %reduce-scatter.4.cloned.1.call-start = ((), (), s32[]{:S(2)}) async-start(), calls=%async_computation.2 | async-start | bytes 589824
  50.0 46.1 %copy-start = (bf16[512,1024]{1,0:T(8,128)(2,1)S(1)}, bf16[512,1024]{1,0:T(8,128)(2,1)}, u32[]{:S(2)}) copy-start(bf16[512,1024]{1,0:T(8,128)(2,1)} %all-gather.2.cloned.1.call-done) | copy-start | bytes 3145732
Sparse Core Ops, SparseCore 0:
  8.9 19.4 all-gather.1
  97.7 59.8 reduce-scatter.3
where the time goes:
time: 166 us
  blocking collectives  80.9 us (49%)
  waiting for transfers between devices  60.8 us (37%)
  between operations  13.5 us (8%)
  matrix products  5.76 us (3%)
  local copies, waits for them, and re-layouts  3.44 us (2%)
  other arithmetic  1.77 us (1%)
    unnamed x3, waiting for transfers between devices  60.8 us
    psum x1, blocking collectives, on_device(): screen_band = lax.psum(screen_part, 'isdf')  37.2 us
    all_gather x1, blocking collectives, on_device(): piece = lax.all_gather(trial, 'isdf', axis=0, tiled=True)  32.7 us
    psum x1, blocking collectives, on_device(): projected = lax.psum(partial_proj, 'band')  5.76 us
    all_gather x1, blocking collectives, on_device(): screen_full = lax.all_gather(screen_band, 'band', axis=1, tiled=True)  5.23 us
    dot_general x1, matrix products, on_device(): screen_part = jnp.dot(rounded, masked, preferred_element_type=jnp.float32)  3.61 us
  transfers between devices with their start and end apart: 2, of which 1 were waited for; matrix products, arithmetic and copies ran while one was open for 1% of the time, Pallas kernels for 0%

commit v1 on v0

v1 whole, which is shorter than its diff:
```python
import functools

import jax
import jax.numpy as jnp
from jax import lax
from jax.experimental import pallas as pl
from jax.experimental.pallas import tpu as pltpu
from jax.sharding import PartitionSpec as P

F32 = jnp.float32
BF16 = jnp.bfloat16


def remote(src, dst, send_sem, recv_sem, band, isdf):
    return pltpu.make_async_remote_copy(
        src_ref=src,
        dst_ref=dst,
        send_sem=send_sem,
        recv_sem=recv_sem,
        device_id=(band, isdf),
        device_id_type=pl.DeviceIdType.MESH,
    )


def body(
    nb, n, nt, r, R,
    trial_ref, cond_ref, val_ref, kern_ref, mask_ref, out_ref,
    trial_my, trial_all, cond_all, val_all, kern_v, q_ref, proj_all, screen_my,
    screen_all, w_ref, red_my, red_all, mix, lsem,
    cond_s, cond_r, val_s, val_r, trial_s, trial_r, proj_s, proj_r,
    screen_s, screen_r, red_s, red_r,
):
    b = lax.axis_index("band")
    i = lax.axis_index("isdf")
    k = lax.rem(b, 2)
    g = b // 2
    ng = nb // 2
    rows, points = cond_ref.shape
    crow = rows // r
    vrow = val_ref.shape[0]
    npc = ng * r
    home = lax.rem(i // r, 2)
    slot = (i // (2 * r)) * r + lax.rem(i, r)
    mine = home == k

    def piece_isdf(p):
        return r * (2 * (p // r) + k) + p % r

    kern_cp = pltpu.make_async_copy(kern_ref, kern_v, lsem.at[0])
    own_cond = pltpu.make_async_copy(cond_ref, cond_all.at[g], lsem.at[1])
    own_val = pltpu.make_async_copy(
        val_ref, val_all.at[pl.ds(pl.multiple_of(k * vrow, vrow), vrow)], lsem.at[2])
    own_val.start()
    own_cond.start()
    kern_cp.start()

    barrier = pltpu.get_barrier_semaphore()

    def greet(bb, ii):
        pl.semaphore_signal(barrier, inc=1, device_id=(bb, ii),
                            device_id_type=pl.DeviceIdType.MESH)

    for d in range(1, nb):
        greet(lax.rem(b + d, nb), i)
    for p in range(npc):
        for c in range(2):
            ip = piece_isdf(p)
            @pl.when(jnp.logical_or(ip != i, k != c))
            def _():
                greet(2 * g + c, ip)
    for d in range(n):
        ii = lax.rem(i + d, n)
        sb = i // R
        if d == 0:
            @pl.when(sb != b)
            def _():
                greet(sb, ii)
            @pl.when(jnp.logical_not(mine))
            def _():
                greet(2 * g + home, ii)
        else:
            greet(sb, ii)
            greet(2 * g + home, ii)

    mix[...] = trial_ref[...].astype(F32)
    for t in range(nt):
        trial_my[t] = mix[pl.ds(t, crow, stride=nt), :].astype(BF16)
    vcols = pl.ds(pl.multiple_of(k * vrow, vrow), vrow)

    @pl.when(mine)
    def _():
        trial_all[slot, :, :, vcols] = trial_my[...]

    total = (nb - 1) + n + nb * R + npc * 2
    selfs = 2 * jnp.where(mine, 1, 0) + jnp.where(i // R == b, 1, 0)
    pl.semaphore_wait(barrier, total - selfs)

    conds = []
    for h in range(r):
        for d in range(1, ng):
            gg = lax.rem(g + d, ng)
            cp = remote(cond_ref.at[pl.ds(h * crow, crow)],
                        cond_all.at[g, pl.ds(h * crow, crow)],
                        cond_s.at[d, h], cond_r.at[g, h], 2 * gg + k, i)
            cp.start()
            conds.append(cp)
    trials = []
    for d in list(range(1, n)) + [0]:
        ii = lax.rem(i + d, n)
        cp = remote(trial_my, trial_all.at[slot, :, :, vcols],
                    trial_s.at[d], trial_r.at[slot, k], 2 * g + home, ii)
        trials.append(cp)
        if d == 0:
            pl.when(jnp.logical_not(mine))(cp.start)
        else:
            cp.start()
    val_cp = remote(val_ref, val_all.at[pl.ds(pl.multiple_of(k * vrow, vrow), vrow)],
                    val_s, val_r, 2 * g + (1 - k), i)
    val_cp.start()

    own_val.wait()
    val_cp.wait_recv()
    for p in range(npc):
        for c in range(2):
            @pl.when(jnp.logical_or(piece_isdf(p) != i, k != c))
            def _():
                remote(trial_my, trial_all.at[p, :, :, pl.ds(c * vrow, vrow)],
                       trial_s.at[0], trial_r.at[p, c], b, i).wait_recv()
        lhs = trial_all[p].reshape(nt * crow, 2 * vrow)
        q_ref[p] = jnp.dot(lhs, val_all[...], preferred_element_type=F32)

    width = 256
    acc = None
    own_cond.wait()
    proj_all[b] = jnp.zeros((nt, points), F32)
    for d in range(ng):
        gg = lax.rem(g + d, ng)
        for h in range(r):
            if d > 0:
                remote(cond_ref.at[pl.ds(h * crow, crow)],
                       cond_all.at[gg, pl.ds(h * crow, crow)],
                       cond_s.at[d, h], cond_r.at[gg, h], b, i).wait_recv()
            for j in range(points // width):
                cols = pl.ds(j * width, width)
                cb = cond_all[gg, pl.ds(h * crow, crow), cols].astype(F32)
                for t in range(nt):
                    x = q_ref[gg * r + h, pl.ds(t * crow, crow), cols] * cb
                    proj_all[b, pl.ds(t, 1), cols] += jnp.sum(x, axis=0, keepdims=True)

    projs = []
    for d in range(1, nb):
        bb = lax.rem(b + d, nb)
        cp = remote(proj_all.at[b], proj_all.at[b], proj_s.at[d], proj_r.at[b], bb, i)
        cp.start()
        projs.append(cp)

    mrows, mcols = mask_ref.shape
    blk = points // mrows
    cols_dev = kern_ref.shape[1]
    spread = (lax.broadcasted_iota(jnp.int32, (mcols, cols_dev), 1) // blk
              == lax.broadcasted_iota(jnp.int32, (mcols, cols_dev), 0))
    keep = jnp.dot((mask_ref[...] > 0).astype(F32).astype(BF16),
                   spread.astype(F32).astype(BF16), preferred_element_type=F32)
    here = (lax.broadcasted_iota(jnp.int32, (mrows, points), 1) // blk
            == lax.broadcasted_iota(jnp.int32, (mrows, points), 0))
    kern_cp.wait()

    for d in range(1, nb):
        bb = lax.rem(b + d, nb)
        remote(proj_all.at[bb], proj_all.at[bb], proj_s.at[d], proj_r.at[bb], b, i).wait_recv()
    proj = proj_all[0]
    for s in range(1, nb):
        proj = proj + proj_all[s]
    lhs = jnp.concatenate(
        [jnp.where(here, proj[t:t + 1], 0.0) for t in range(nt)], axis=0).astype(BF16)
    scr = jnp.dot(lhs, kern_v[...], preferred_element_type=F32)
    for t in range(nt):
        s = jnp.sum(scr[t * mrows:(t + 1) * mrows] * keep, axis=0, keepdims=True)
        for h in range(R):
            screen_my[h, pl.ds(t, 1), :] = s[:, h * points:(h + 1) * points]

    screens = []
    for h in range(R):
        ii = R * b + h
        for d in range(nb):
            bb = lax.rem(b + d, nb)
            cp = remote(screen_my.at[h], screen_all.at[i], screen_s.at[h, d],
                        screen_r.at[i], bb, ii)
            if d == 0:
                away = ii != i
                pl.when(away)(cp.start)

                @pl.when(jnp.logical_not(away))
                def _():
                    screen_all[i] = screen_my[h]
                screens.append((cp, away))
            else:
                cp.start()
                screens.append((cp, None))

    for d in range(n):
        ii = lax.rem(i + d, n)
        cp = remote(screen_my.at[0], screen_all.at[ii], screen_s.at[0, 0],
                    screen_r.at[ii], b, i)
        if d == 0:
            pl.when(i // R != b)(cp.wait_recv)
        else:
            cp.wait_recv()
    scr = screen_all[0]
    for s in range(1, n):
        scr = scr + screen_all[s]

    for t in range(nt):
        w_ref[pl.ds(t * 2 * vrow, 2 * vrow)] = (
            val_all[...].astype(F32) * scr[t:t + 1]).astype(BF16)
    reds = []
    for gg in range(ng):
        part = lax.dot_general(cond_all[gg], w_ref[...], (((1,), (1,)), ((), ())),
                               preferred_element_type=F32).astype(BF16)
        for h in range(r):
            p = gg * r + h
            ii = piece_isdf(p)
            for c in range(2):
                for t in range(nt):
                    lo = t * 2 * vrow + c * vrow
                    red_my[p, c, t] = part[h * crow:(h + 1) * crow, lo:lo + vrow]
                cp = remote(red_my.at[p, c], red_all.at[i], red_s.at[p, c],
                            red_r.at[i], 2 * g + c, ii)
                away = jnp.logical_or(ii != i, k != c)
                pl.when(away)(cp.start)

                @pl.when(jnp.logical_not(away))
                def _():
                    red_all[i] = red_my[p, c]
                reds.append((cp, away))

    for d in range(n):
        ii = lax.rem(i + d, n)
        cp = remote(red_my.at[0, 0], red_all.at[ii], red_s.at[0, 0], red_r.at[ii], b, i)
        if d == 0:
            pl.when(jnp.logical_not(mine))(cp.wait_recv)
        else:
            cp.wait_recv()
    for t in range(nt):
        tot = red_all[0, t].astype(F32)
        for s in range(1, n):
            tot = tot + red_all[s, t].astype(F32)
        mix[pl.ds(t, crow, stride=nt), :] = tot
    out_ref[...] = mix[...].astype(BF16)

    for cp in conds + projs + [val_cp]:
        cp.wait_send()
    for cp in trials[:-1]:
        cp.wait_send()
    pl.when(jnp.logical_not(mine))(trials[-1].wait_send)
    for cp, away in screens + reds:
        if away is None:
            cp.wait_send()
        else:
            pl.when(away)(cp.wait_send)


def on_device(nb, n, trial, cond_coef, val_coef, kernel, block_mask):
    crow, nt, vrow = trial.shape
    rows, points = cond_coef.shape
    r = rows // crow
    R = kernel.shape[1] // points
    ng = nb // 2
    npc = ng * r
    dma = pltpu.SemaphoreType.DMA
    anyspec = pl.BlockSpec(memory_space=pl.ANY)
    vspec = pl.BlockSpec(memory_space=pltpu.VMEM)
    out = pl.pallas_call(
        functools.partial(body, nb, n, nt, r, R),
        out_shape=jax.ShapeDtypeStruct((crow * nt, vrow), BF16),
        in_specs=[vspec, anyspec, anyspec, anyspec, vspec],
        out_specs=vspec,
        scratch_shapes=[
            pltpu.VMEM((nt, crow, vrow), BF16),
            pltpu.VMEM((npc, nt, crow, 2 * vrow), BF16),
            pltpu.VMEM((ng, rows, points), BF16),
            pltpu.VMEM((2 * vrow, points), BF16),
            pltpu.VMEM(kernel.shape, BF16),
            pltpu.VMEM((npc, nt * crow, points), F32),
            pltpu.VMEM((nb, nt, points), F32),
            pltpu.VMEM((R, nt, points), F32),
            pltpu.VMEM((n, nt, points), F32),
            pltpu.VMEM((nt * 2 * vrow, points), BF16),
            pltpu.VMEM((npc, 2, nt, crow, vrow), BF16),
            pltpu.VMEM((n, nt, crow, vrow), BF16),
            pltpu.VMEM((nt * crow, vrow), F32),
            dma((3,)),
            dma((ng, r)), dma((ng, r)),
            dma, dma,
            dma((n,)), dma((npc, 2)),
            dma((nb,)), dma((nb,)),
            dma((R, nb)), dma((n,)),
            dma((npc, 2)), dma((n,)),
        ],
        compiler_params=pltpu.CompilerParams(
            collective_id=0, has_side_effects=True, vmem_limit_bytes=50 * 1024 * 1024),
        name="sigma_product",
    )(trial.reshape(crow * nt, vrow), cond_coef, val_coef, kernel, block_mask)
    return out.reshape(trial.shape)


def solution(mesh):
    return jax.shard_map(
        functools.partial(on_device, mesh.shape["band"], mesh.shape["isdf"]),
        mesh=mesh,
        in_specs=(
            P("isdf", None, "band"),
            P("band", "isdf"),
            P("band", "isdf"),
            P("isdf", "band"),
            P("isdf", "band"),
        ),
        out_specs=P("isdf", None, "band"),
        check_vma=False,
    )
```

time: 166 us -> 35 us (0.21)
  blocking collectives: 80.9 us -> 0 us
  waiting for transfers between devices: 60.8 us -> 0 us
  Pallas kernels: 0 us -> 30.7 us
  between operations: 13.5 us -> 0.01 us
  matrix products: 5.76 us -> 0 us
  other arithmetic: 1.77 us -> 0 us
    unnamed x3 -> x0, waiting for transfers between devices: 60.8 us -> none
    psum x2 -> x0, blocking collectives: 42.9 us -> none  [the longest x1 37.2 us: on_device(): screen_band = lax.psum(screen_part, 'isdf')]
    all_gather x2 -> x0, blocking collectives: 38 us -> none  [the longest x1 32.7 us: on_device(): piece = lax.all_gather(trial, 'isdf', axis=0, tiled=True)]
    pallas_call x0 -> x1, Pallas kernels: none -> 30.7 us  [on_device(): pl.pallas_call(functools.partial(body, nb, n, nt, r, R), out_shape=jax.Sh...]
    dot_general x3 -> x0, matrix products: 5.76 us -> none  [the longest x1 3.61 us: on_device(): screen_part = jnp.dot(rounded, masked, preferred_element_type=jnp.float32)]
    unnamed x4 -> x9, local copies, waits for them, and re-layouts: 1.95 us -> 3.96 us
  transfers between devices with their start and end apart: 2 -> 0, of which waited for: 1 -> 0; matrix products, arithmetic and copies ran while one was open for 1% -> 0% of each run, Pallas kernels for 0% -> 0%
where the time goes in v1:
time: 35 us; the launch traced here: 34.6 us
  Pallas kernels  30.7 us (88%)
  local copies, waits for them, and re-layouts  3.96 us (11%)
    pallas_call x1, Pallas kernels, on_device(): pl.pallas_call(functools.partial(body, nb, n, nt, r, R), out_shape=jax.Sh...  30.7 us
    unnamed x9, local copies, waits for them, and re-layouts  3.96 us

profile of v1, /device:TPU:0, one launch (start us, length us, event | category | flops | bytes accessed | tf_op | source)
XLA Modules:
  0.0 34.6 jit_solution(12417918460010183254)
XLA Ops:
  0.0 0.0 copy-start
  0.0 0.9 %copy-done = bf16[128,1024]{1,0:T(8,128)(2,1)S(1)} copy-done((bf16[128,1024]{1,0:T(8,128)(2,1)S(1)}, bf16[128,1024]{1,0:T(8,128)(2,1)}, u32[]{:S(2)}) %copy-start) | copy-done | bytes 262168
  1.0 0.0 copy-start.1
  1.0 0.9 %copy-done.1 = bf16[128,1024]{1,0:T(8,128)(2,1)S(1)} copy-done((bf16[128,1024]{1,0:T(8,128)(2,1)S(1)}, bf16[128,1024]{1,0:T(8,128)(2,1)}, u32[]{:S(2)}) %copy-start.1) | copy-done | bytes 262168
  1.9 0.0 copy-start.2
  1.9 0.8 %copy-done.2 = bf16[64,2,128]{2,1,0:T(2,128)(2,1)S(1)} copy-done((bf16[64,2,128]{2,1,0:T(2,128)(2,1)S(1)}, bf16[64,2,128]{2,1,0:T(2,128)(2,1)}, u32[]{:S(2)}) %copy-start.2) | copy-done | bytes 32792
  2.7 0.0 copy-start.3
  2.7 0.7 %copy-done.3 = s32[8,16]{1,0:T(8,128)S(1)} copy-done((s32[8,16]{1,0:T(8,128)S(1)}, s32[8,16]{1,0:T(8,128)}, u32[]{:S(2)}) %copy-start.3) | copy-done | bytes 536
  3.3 30.7 %sigma_product.1 = bf16[128,128]{1,0:T(8,128)(2,1)S(1)} custom-call(bf16[128,128]{1,0:T(8,128)(2,1)S(1)} %bitcast.3, bf16[128,1024]{1,0:T(8,128)(2,1)S(1)} %copy-done, bf16[128,1024]{1,0:T(8,128)(2,1)S(1)} %copy-done.1, bf16[1024,2048]{1,0:T(8,128)(2,1)} %kern_ref.1, s32[8,16]{1,0:T(8,128)S(1)} %copy-done.3), custom_call_target="tpu_custom_call" | custom-call | tf_op jit(solution)/shard_map/sigma_product/pallas_call | solution.py:273
  34.0 0.6 %copy.7 = bf16[64,2,128]{2,1,0:T(2,128)(2,1)} copy(bf16[64,2,128]{2,1,0:T(2,128)(2,1)S(1)} %bitcast.2) | data formatting | bytes 65536
Async XLA Ops:
  0.0 0.9 %copy-start = (bf16[128,1024]{1,0:T(8,128)(2,1)S(1)}, bf16[128,1024]{1,0:T(8,128)(2,1)}, u32[]{:S(2)}) copy-start(bf16[128,1024]{1,0:T(8,128)(2,1)} %cond_ref.1) | copy-start | bytes 786436
  1.0 0.9 %copy-start.1 = (bf16[128,1024]{1,0:T(8,128)(2,1)S(1)}, bf16[128,1024]{1,0:T(8,128)(2,1)}, u32[]{:S(2)}) copy-start(bf16[128,1024]{1,0:T(8,128)(2,1)} %val_ref.1) | copy-start | bytes 786436
  1.9 0.8 %copy-start.2 = (bf16[64,2,128]{2,1,0:T(2,128)(2,1)S(1)}, bf16[64,2,128]{2,1,0:T(2,128)(2,1)}, u32[]{:S(2)}) copy-start(bf16[64,2,128]{2,1,0:T(2,128)(2,1)} %param.5) | copy-start | bytes 98308
  2.7 0.7 %copy-start.3 = (s32[8,16]{1,0:T(8,128)S(1)}, s32[8,16]{1,0:T(8,128)}, u32[]{:S(2)}) copy-start(s32[8,16]{1,0:T(8,128)} %mask_ref.1) | copy-start | bytes 1540

commit v2 on v1

--- a/solution.py
+++ b/solution.py
@@ -25,7 +25,7 @@
 def body(
     nb, n, nt, r, R,
     trial_ref, cond_ref, val_ref, kern_ref, mask_ref, out_ref,
-    trial_my, trial_all, cond_all, val_all, kern_v, q_ref, proj_all, screen_my,
+    trial_in, mask_in, trial_my, trial_all, cond_all, val_all, kern_v, q_ref, acc_ref, proj_all, screen_my,
     screen_all, w_ref, red_my, red_all, mix, lsem,
     cond_s, cond_r, val_s, val_r, trial_s, trial_r, proj_s, proj_r,
     screen_s, screen_r, red_s, red_r,
@@ -46,43 +46,35 @@
     def piece_isdf(p):
         return r * (2 * (p // r) + k) + p % r
 
+    barrier = pltpu.get_barrier_semaphore()
+
+    def greet(bb, ii):
+        pl.semaphore_signal(barrier, inc=1, device_id=(bb, ii),
+                            device_id_type=pl.DeviceIdType.MESH)
+
+    for p in range(npc):
+        for c in range(2):
+            ip = piece_isdf(p)
+            @pl.when(ip != i)
+            def _():
+                greet(2 * g + c, ip)
+    for d in range(1, nb):
+        greet(lax.rem(b + d, nb), i)
+
     kern_cp = pltpu.make_async_copy(kern_ref, kern_v, lsem.at[0])
     own_cond = pltpu.make_async_copy(cond_ref, cond_all.at[g], lsem.at[1])
     own_val = pltpu.make_async_copy(
         val_ref, val_all.at[pl.ds(pl.multiple_of(k * vrow, vrow), vrow)], lsem.at[2])
+    trial_cp = pltpu.make_async_copy(trial_ref, trial_in, lsem.at[3])
+    mask_cp = pltpu.make_async_copy(mask_ref, mask_in, lsem.at[4])
+    trial_cp.start()
     own_val.start()
     own_cond.start()
+    mask_cp.start()
     kern_cp.start()
 
-    barrier = pltpu.get_barrier_semaphore()
-
-    def greet(bb, ii):
-        pl.semaphore_signal(barrier, inc=1, device_id=(bb, ii),
-                            device_id_type=pl.DeviceIdType.MESH)
-
-    for d in range(1, nb):
-        greet(lax.rem(b + d, nb), i)
-    for p in range(npc):
-        for c in range(2):
-            ip = piece_isdf(p)
-            @pl.when(jnp.logical_or(ip != i, k != c))
-            def _():
-                greet(2 * g + c, ip)
-    for d in range(n):
-        ii = lax.rem(i + d, n)
-        sb = i // R
-        if d == 0:
-            @pl.when(sb != b)
-            def _():
-                greet(sb, ii)
-            @pl.when(jnp.logical_not(mine))
-            def _():
-                greet(2 * g + home, ii)
-        else:
-            greet(sb, ii)
-            greet(2 * g + home, ii)
-
-    mix[...] = trial_ref[...].astype(F32)
+    trial_cp.wait()
+    mix[...] = trial_in[...].astype(F32)
     for t in range(nt):
         trial_my[t] = mix[pl.ds(t, crow, stride=nt), :].astype(BF16)
     vcols = pl.ds(pl.multiple_of(k * vrow, vrow), vrow)
@@ -91,11 +83,13 @@
     def _():
         trial_all[slot, :, :, vcols] = trial_my[...]
 
-    total = (nb - 1) + n + nb * R + npc * 2
-    selfs = 2 * jnp.where(mine, 1, 0) + jnp.where(i // R == b, 1, 0)
-    pl.semaphore_wait(barrier, total - selfs)
-
-    conds = []
+    pl.semaphore_wait(barrier, nb - 1 + n - 1)
+
+    pending = []
+    val_cp = remote(val_ref, val_all.at[pl.ds(pl.multiple_of(k * vrow, vrow), vrow)],
+                    val_s, val_r, 2 * g + (1 - k), i)
+    val_cp.start()
+    pending.append(val_cp.wait_send)
     for h in range(r):
         for d in range(1, ng):
             gg = lax.rem(g + d, ng)
@@ -103,20 +97,17 @@
                         cond_all.at[g, pl.ds(h * crow, crow)],
                         cond_s.at[d, h], cond_r.at[g, h], 2 * gg + k, i)
             cp.start()
-            conds.append(cp)
-    trials = []
+            pending.append(cp.wait_send)
     for d in list(range(1, n)) + [0]:
         ii = lax.rem(i + d, n)
         cp = remote(trial_my, trial_all.at[slot, :, :, vcols],
                     trial_s.at[d], trial_r.at[slot, k], 2 * g + home, ii)
-        trials.append(cp)
         if d == 0:
             pl.when(jnp.logical_not(mine))(cp.start)
+            pending.append(functools.partial(pl.when(jnp.logical_not(mine)), cp.wait_send))
         else:
             cp.start()
-    val_cp = remote(val_ref, val_all.at[pl.ds(pl.multiple_of(k * vrow, vrow), vrow)],
-                    val_s, val_r, 2 * g + (1 - k), i)
-    val_cp.start()
+            pending.append(cp.wait_send)
 
     own_val.wait()
     val_cp.wait_recv()
@@ -126,13 +117,15 @@
             def _():
                 remote(trial_my, trial_all.at[p, :, :, pl.ds(c * vrow, vrow)],
                        trial_s.at[0], trial_r.at[p, c], b, i).wait_recv()
-        lhs = trial_all[p].reshape(nt * crow, 2 * vrow)
-        q_ref[p] = jnp.dot(lhs, val_all[...], preferred_element_type=F32)
+        if p % r == r - 1:
+            lo = p - r + 1
+            lhs = trial_all[lo:p + 1].reshape(r * nt * crow, 2 * vrow)
+            q_ref[lo:p + 1] = jnp.dot(
+                lhs, val_all[...], preferred_element_type=F32
+            ).reshape(r, nt * crow, points)
 
     width = 256
-    acc = None
     own_cond.wait()
-    proj_all[b] = jnp.zeros((nt, points), F32)
     for d in range(ng):
         gg = lax.rem(g + d, ng)
         for h in range(r):
@@ -145,21 +138,27 @@
                 cb = cond_all[gg, pl.ds(h * crow, crow), cols].astype(F32)
                 for t in range(nt):
                     x = q_ref[gg * r + h, pl.ds(t * crow, crow), cols] * cb
-                    proj_all[b, pl.ds(t, 1), cols] += jnp.sum(x, axis=0, keepdims=True)
-
-    projs = []
+                    x = jnp.sum(x.reshape(crow // 8, 8, width), axis=0)
+                    if d == 0 and h == 0:
+                        acc_ref[t, :, cols] = x
+                    else:
+                        acc_ref[t, :, cols] += x
+    for t in range(nt):
+        proj_all[b, pl.ds(t, 1), :] = jnp.sum(acc_ref[t], axis=0, keepdims=True)
+
     for d in range(1, nb):
         bb = lax.rem(b + d, nb)
         cp = remote(proj_all.at[b], proj_all.at[b], proj_s.at[d], proj_r.at[b], bb, i)
         cp.start()
-        projs.append(cp)
-
+        pending.append(cp.wait_send)
+
+    mask_cp.wait()
     mrows, mcols = mask_ref.shape
     blk = points // mrows
     cols_dev = kern_ref.shape[1]
     spread = (lax.broadcasted_iota(jnp.int32, (mcols, cols_dev), 1) // blk
               == lax.broadcasted_iota(jnp.int32, (mcols, cols_dev), 0))
-    keep = jnp.dot((mask_ref[...] > 0).astype(F32).astype(BF16),
+    keep = jnp.dot((mask_in[...] > 0).astype(F32).astype(BF16),
                    spread.astype(F32).astype(BF16), preferred_element_type=F32)
     here = (lax.broadcasted_iota(jnp.int32, (mrows, points), 1) // blk
             == lax.broadcasted_iota(jnp.int32, (mrows, points), 0))
@@ -179,7 +178,6 @@
         for h in range(R):
             screen_my[h, pl.ds(t, 1), :] = s[:, h * points:(h + 1) * points]
 
-    screens = []
     for h in range(R):
         ii = R * b + h
         for d in range(nb):
@@ -193,10 +191,10 @@
                 @pl.when(jnp.logical_not(away))
                 def _():
                     screen_all[i] = screen_my[h]
-                screens.append((cp, away))
+                pending.append(functools.partial(pl.when(away), cp.wait_send))
             else:
                 cp.start()
-                screens.append((cp, None))
+                pending.append(cp.wait_send)
 
     for d in range(n):
         ii = lax.rem(i + d, n)
@@ -213,7 +211,6 @@
     for t in range(nt):
         w_ref[pl.ds(t * 2 * vrow, 2 * vrow)] = (
             val_all[...].astype(F32) * scr[t:t + 1]).astype(BF16)
-    reds = []
     for gg in range(ng):
         part = lax.dot_general(cond_all[gg], w_ref[...], (((1,), (1,)), ((), ())),
                                preferred_element_type=F32).astype(BF16)
@@ -232,7 +229,7 @@
                 @pl.when(jnp.logical_not(away))
                 def _():
                     red_all[i] = red_my[p, c]
-                reds.append((cp, away))
+                pending.append(functools.partial(pl.when(away), cp.wait_send))
 
     for d in range(n):
         ii = lax.rem(i + d, n)
@@ -248,16 +245,8 @@
         mix[pl.ds(t, crow, stride=nt), :] = tot
     out_ref[...] = mix[...].astype(BF16)
 
-    for cp in conds + projs + [val_cp]:
-        cp.wait_send()
-    for cp in trials[:-1]:
-        cp.wait_send()
-    pl.when(jnp.logical_not(mine))(trials[-1].wait_send)
-    for cp, away in screens + reds:
-        if away is None:
-            cp.wait_send()
-        else:
-            pl.when(away)(cp.wait_send)
+    for wait in pending:
+        wait()
 
 
 def on_device(nb, n, trial, cond_coef, val_coef, kernel, block_mask):
@@ -268,20 +257,23 @@
     ng = nb // 2
     npc = ng * r
     dma = pltpu.SemaphoreType.DMA
-    anyspec = pl.BlockSpec(memory_space=pl.ANY)
+    hbm = pl.BlockSpec(memory_space=pltpu.HBM)
     vspec = pl.BlockSpec(memory_space=pltpu.VMEM)
     out = pl.pallas_call(
         functools.partial(body, nb, n, nt, r, R),
         out_shape=jax.ShapeDtypeStruct((crow * nt, vrow), BF16),
-        in_specs=[vspec, anyspec, anyspec, anyspec, vspec],
+        in_specs=[hbm, hbm, hbm, hbm, hbm],
         out_specs=vspec,
         scratch_shapes=[
+            pltpu.VMEM((crow * nt, vrow), BF16),
+            pltpu.VMEM(block_mask.shape, jnp.int32),
             pltpu.VMEM((nt, crow, vrow), BF16),
             pltpu.VMEM((npc, nt, crow, 2 * vrow), BF16),
             pltpu.VMEM((ng, rows, points), BF16),
             pltpu.VMEM((2 * vrow, points), BF16),
             pltpu.VMEM(kernel.shape, BF16),
             pltpu.VMEM((npc, nt * crow, points), F32),
+            pltpu.VMEM((nt, 8, points), F32),
             pltpu.VMEM((nb, nt, points), F32),
             pltpu.VMEM((R, nt, points), F32),
             pltpu.VMEM((n, nt, points), F32),
@@ -289,7 +281,7 @@
             pltpu.VMEM((npc, 2, nt, crow, vrow), BF16),
             pltpu.VMEM((n, nt, crow, vrow), BF16),
             pltpu.VMEM((nt * crow, vrow), F32),
-            dma((3,)),
+            dma((5,)),
             dma((ng, r)), dma((ng, r)),
             dma, dma,
             dma((n,)), dma((npc, 2)),
@@ -298,7 +290,7 @@
             dma((npc, 2)), dma((n,)),
         ],
         compiler_params=pltpu.CompilerParams(
-            collective_id=0, has_side_effects=True, vmem_limit_bytes=50 * 1024 * 1024),
+            collective_id=0, has_side_effects=True, vmem_limit_bytes=63 * 1024 * 1024),
         name="sigma_product",
     )(trial.reshape(crow * nt, vrow), cond_coef, val_coef, kernel, block_mask)
     return out.reshape(trial.shape)

time: 35 us -> 32.4 us (0.926)
  local copies, waits for them, and re-layouts: 3.96 us -> 1.4 us
    unnamed x9 -> x1, local copies, waits for them, and re-layouts: 3.96 us -> 1.4 us
where the time goes in v2:
time: 32.4 us; the launch traced here: 32.2 us
  Pallas kernels  30.8 us (95%)
  local copies, waits for them, and re-layouts  1.4 us (4%)
    pallas_call x1, Pallas kernels, on_device(): pl.pallas_call(functools.partial(body, nb, n, nt, r, R), out_shape=jax.Sh...  30.8 us
    unnamed x1, local copies, waits for them, and re-layouts  1.4 us

profile of v2, /device:TPU:0, one launch (start us, length us, event | category | flops | bytes accessed | tf_op | source)
XLA Modules:
  0.0 32.2 jit_solution(7736081639538843134)
XLA Ops:
  0.0 30.8 %sigma_product.1 = bf16[128,128]{1,0:T(8,128)(2,1)} custom-call(bf16[128,128]{1,0:T(8,128)(2,1)} %bitcast.3, bf16[128,1024]{1,0:T(8,128)(2,1)} %cond_ref.1, bf16[128,1024]{1,0:T(8,128)(2,1)} %val_ref.1, bf16[1024,2048]{1,0:T(8,128)(2,1)} %kern_ref.1, s32[8,16]{1,0:T(8,128)} %mask_ref.1), custom_call_target="tpu_custom_call" | custom-call | tf_op jit(solution)/shard_map/sigma_product/pallas_call | solution.py:262
  30.8 1.4 %copy.7 = bf16[64,2,128]{2,1,0:T(2,128)(2,1)} copy(bf16[64,2,128]{2,1,0:T(2,128)(2,1)} %bitcast.2) | data formatting | bytes 65536

commit v3 on v2

--- a/solution.py
+++ b/solution.py
@@ -178,23 +178,24 @@
         for h in range(R):
             screen_my[h, pl.ds(t, 1), :] = s[:, h * points:(h + 1) * points]
 
-    for h in range(R):
-        ii = R * b + h
-        for d in range(nb):
-            bb = lax.rem(b + d, nb)
-            cp = remote(screen_my.at[h], screen_all.at[i], screen_s.at[h, d],
-                        screen_r.at[i], bb, ii)
-            if d == 0:
-                away = ii != i
-                pl.when(away)(cp.start)
-
-                @pl.when(jnp.logical_not(away))
-                def _():
-                    screen_all[i] = screen_my[h]
-                pending.append(functools.partial(pl.when(away), cp.wait_send))
-            else:
-                cp.start()
-                pending.append(cp.wait_send)
+    for e in list(range(1, ng)) + [0]:
+        for h in range(R):
+            ii = R * b + h
+            for c in range(2):
+                bb = 2 * lax.rem(g + e, ng) + lax.rem(k + 1 + c, 2)
+                cp = remote(screen_my.at[h], screen_all.at[i], screen_s.at[h, 2 * e + c],
+                            screen_r.at[i], bb, ii)
+                if e == 0 and c == 1:
+                    away = ii != i
+                    pl.when(away)(cp.start)
+
+                    @pl.when(jnp.logical_not(away))
+                    def _():
+                        screen_all[i] = screen_my[h]
+                    pending.append(functools.partial(pl.when(away), cp.wait_send))
+                else:
+                    cp.start()
+                    pending.append(cp.wait_send)
 
     for d in range(n):
         ii = lax.rem(i + d, n)
@@ -211,16 +212,20 @@
     for t in range(nt):
         w_ref[pl.ds(t * 2 * vrow, 2 * vrow)] = (
             val_all[...].astype(F32) * scr[t:t + 1]).astype(BF16)
-    for gg in range(ng):
+    for e in range(ng):
+        gg = lax.rem(i // (2 * r) + 1 + e, ng)
         part = lax.dot_general(cond_all[gg], w_ref[...], (((1,), (1,)), ((), ())),
                                preferred_element_type=F32).astype(BF16)
         for h in range(r):
-            p = gg * r + h
-            ii = piece_isdf(p)
             for c in range(2):
                 for t in range(nt):
                     lo = t * 2 * vrow + c * vrow
-                    red_my[p, c, t] = part[h * crow:(h + 1) * crow, lo:lo + vrow]
+                    red_my[gg * r + h, c, t] = part[h * crow:(h + 1) * crow, lo:lo + vrow]
+        for q in range(r):
+            h = lax.rem(i + 1 + q, r)
+            p = gg * r + h
+            ii = r * (2 * gg + k) + h
+            for c in range(2):
                 cp = remote(red_my.at[p, c], red_all.at[i], red_s.at[p, c],
                             red_r.at[i], 2 * g + c, ii)
                 away = jnp.logical_or(ii != i, k != c)
@@ -261,7 +266,7 @@
     vspec = pl.BlockSpec(memory_space=pltpu.VMEM)
     out = pl.pallas_call(
         functools.partial(body, nb, n, nt, r, R),
-        out_shape=jax.ShapeDtypeStruct((crow * nt, vrow), BF16),
+        out_shape=pltpu.VMEM((crow * nt, vrow), BF16),
         in_specs=[hbm, hbm, hbm, hbm, hbm],
         out_specs=vspec,
         scratch_shapes=[

time: 32.4 us -> 31 us (0.957)
  local copies, waits for them, and re-layouts: 1.4 us -> 0.62 us
  Pallas kernels: 30.8 us -> 30.2 us
    unnamed x1, local copies, waits for them, and re-layouts: 1.4 us -> 0.62 us
    pallas_call x1, Pallas kernels: 30.8 us -> 30.2 us  [on_device(): pl.pallas_call(functools.partial(body, nb, n, nt, r, R), out_shape=pltpu....]
where the time goes in v3:
time: 31 us; the launch traced here: 30.9 us
  Pallas kernels  30.2 us (97%)
  local copies, waits for them, and re-layouts  0.62 us (2%)
    pallas_call x1, Pallas kernels, on_device(): pl.pallas_call(functools.partial(body, nb, n, nt, r, R), out_shape=pltpu....  30.2 us

profile of v3, /device:TPU:0, one launch (start us, length us, event | category | flops | bytes accessed | tf_op | source)
XLA Modules:
  0.0 30.9 jit_solution(9068295953720265260)
XLA Ops:
  0.0 30.2 %sigma_product.1 = bf16[128,128]{1,0:T(8,128)(2,1)S(1)} custom-call(bf16[128,128]{1,0:T(8,128)(2,1)} %bitcast.3, bf16[128,1024]{1,0:T(8,128)(2,1)} %cond_ref.1, bf16[128,1024]{1,0:T(8,128)(2,1)} %val_ref.1, bf16[1024,2048]{1,0:T(8,128)(2,1)} %kern_ref.1, s32[8,16]{1,0:T(8,128)} %mask_ref.1), custom_call_target="tpu_custom_call" | custom-call | tf_op jit(solution)/shard_map/sigma_product/pallas_call | solution.py:267
  30.2 0.6 %copy.7 = bf16[64,2,128]{2,1,0:T(2,128)(2,1)} copy(bf16[64,2,128]{2,1,0:T(2,128)(2,1)S(1)} %bitcast.2) | data formatting | bytes 65536

commit v4 on v3

--- a/solution.py
+++ b/solution.py
@@ -86,10 +86,6 @@
     pl.semaphore_wait(barrier, nb - 1 + n - 1)
 
     pending = []
-    val_cp = remote(val_ref, val_all.at[pl.ds(pl.multiple_of(k * vrow, vrow), vrow)],
-                    val_s, val_r, 2 * g + (1 - k), i)
-    val_cp.start()
-    pending.append(val_cp.wait_send)
     for h in range(r):
         for d in range(1, ng):
             gg = lax.rem(g + d, ng)
@@ -98,6 +94,10 @@
                         cond_s.at[d, h], cond_r.at[g, h], 2 * gg + k, i)
             cp.start()
             pending.append(cp.wait_send)
+    val_cp = remote(val_ref, val_all.at[pl.ds(pl.multiple_of(k * vrow, vrow), vrow)],
+                    val_s, val_r, 2 * g + (1 - k), i)
+    val_cp.start()
+    pending.append(val_cp.wait_send)
     for d in list(range(1, n)) + [0]:
         ii = lax.rem(i + d, n)
         cp = remote(trial_my, trial_all.at[slot, :, :, vcols],
@@ -146,11 +146,15 @@
     for t in range(nt):
         proj_all[b, pl.ds(t, 1), :] = jnp.sum(acc_ref[t], axis=0, keepdims=True)
 
-    for d in range(1, nb):
-        bb = lax.rem(b + d, nb)
+    for d in list(range(2, nb)) + [1]:
+        bb = 2 * lax.rem(g + d // 2, ng) + lax.rem(k + d, 2)
         cp = remote(proj_all.at[b], proj_all.at[b], proj_s.at[d], proj_r.at[b], bb, i)
         cp.start()
         pending.append(cp.wait_send)
+
+    for wait in pending[:-(nb - 1)]:
+        wait()
+    del pending[:-(nb - 1)]
 
     mask_cp.wait()
     mrows, mcols = mask_ref.shape
@@ -212,15 +216,15 @@
     for t in range(nt):
         w_ref[pl.ds(t * 2 * vrow, 2 * vrow)] = (
             val_all[...].astype(F32) * scr[t:t + 1]).astype(BF16)
+    part = lax.dot_general(cond_all[...].reshape(ng * rows, points), w_ref[...],
+                           (((1,), (1,)), ((), ())), preferred_element_type=F32).astype(BF16)
+    for p in range(npc):
+        for c in range(2):
+            for t in range(nt):
+                lo = t * 2 * vrow + c * vrow
+                red_my[p, c, t] = part[p * crow:(p + 1) * crow, lo:lo + vrow]
     for e in range(ng):
         gg = lax.rem(i // (2 * r) + 1 + e, ng)
-        part = lax.dot_general(cond_all[gg], w_ref[...], (((1,), (1,)), ((), ())),
-                               preferred_element_type=F32).astype(BF16)
-        for h in range(r):
-            for c in range(2):
-                for t in range(nt):
-                    lo = t * 2 * vrow + c * vrow
-                    red_my[gg * r + h, c, t] = part[h * crow:(h + 1) * crow, lo:lo + vrow]
         for q in range(r):
             h = lax.rem(i + 1 + q, r)
             p = gg * r + h
@@ -236,6 +240,9 @@
                     red_all[i] = red_my[p, c]
                 pending.append(functools.partial(pl.when(away), cp.wait_send))
 
+    for wait in pending:
+        wait()
+    pending.clear()
     for d in range(n):
         ii = lax.rem(i + d, n)
         cp = remote(red_my.at[0, 0], red_all.at[ii], red_s.at[0, 0], red_r.at[ii], b, i)
@@ -249,9 +256,6 @@
             tot = tot + red_all[s, t].astype(F32)
         mix[pl.ds(t, crow, stride=nt), :] = tot
     out_ref[...] = mix[...].astype(BF16)
-
-    for wait in pending:
-        wait()
 
 
 def on_device(nb, n, trial, cond_coef, val_coef, kernel, block_mask):

time: 31 us -> 30.9 us (level)
  no operation moved by 1% of the time
where the time goes in v4:
time: 30.9 us; the launch traced here: 30.8 us
  Pallas kernels  30.2 us (98%)
  local copies, waits for them, and re-layouts  0.62 us (2%)
    pallas_call x1, Pallas kernels, on_device(): pl.pallas_call(functools.partial(body, nb, n, nt, r, R), out_shape=pltpu....  30.2 us

profile of v4, /device:TPU:0, one launch (start us, length us, event | category | flops | bytes accessed | tf_op | source)
XLA Modules:
  0.0 30.8 jit_solution(14790718356375318639)
XLA Ops:
  0.0 30.2 %sigma_product.1 = bf16[128,128]{1,0:T(8,128)(2,1)S(1)} custom-call(bf16[128,128]{1,0:T(8,128)(2,1)} %bitcast.3, bf16[128,1024]{1,0:T(8,128)(2,1)} %cond_ref.1, bf16[128,1024]{1,0:T(8,128)(2,1)} %val_ref.1, bf16[1024,2048]{1,0:T(8,128)(2,1)} %kern_ref.1, s32[8,16]{1,0:T(8,128)} %mask_ref.1), custom_call_target="tpu_custom_call" | custom-call | tf_op jit(solution)/shard_map/sigma_product/pallas_call | solution.py:271
  30.2 0.6 %copy.7 = bf16[64,2,128]{2,1,0:T(2,128)(2,1)} copy(bf16[64,2,128]{2,1,0:T(2,128)(2,1)S(1)} %bitcast.2) | data formatting | bytes 65536
